TPU v7x, 256 devices: a whole 4x4x8 slice. The times are simulated.
256 devices in a mesh: gx: 8 (over z), gy: 16 (over y, x_hi, core), gz: 2 (over x_lo).
Axes of the slice: x: 4 (x_hi: 2, x_lo: 2; x = x_hi * 2 + x_lo), y: 4, z: 8, core: 2. Of those that a mesh axis runs over, the one named last changes fastest.
Arguments:
- density: float32 [64, 1024, 256], P('gx', 'gy', 'gz'), may hold values from 0.5 to 2
- momentum: float32 [3, 64, 1024, 256], P(None, 'gx', 'gy', 'gz'), may hold values from -0.6 to 0.6
- column_shift: int32 [64], replicated, may hold values from 0 to 1023
- column_fraction: float32 [64], replicated, may hold values from 0 to 1
- shear_offset: int32 [1], replicated, may hold values from 0 to 1023
Outputs:
- density_next: float32 [64, 1024, 256], P('gx', 'gy', 'gz')
- momentum_next: float32 [3, 64, 1024, 256], P(None, 'gx', 'gy', 'gz')
All inputs are finite; a program needn't handle non-finite values.
Results may differ from a plain program's by a relative error of at most 0.0003.
Values sent between devices are 32-bit elements; how exact they have to be, the bound alone decides.
No kernel may reach another device: no remote copies, remote signals or barrier semaphores. Data moves between devices by JAX's collectives and lax.ppermute only.
A program may use at most 128 MiB of HBM per device.

v0:
```python
import jax
import jax.numpy as jnp
from jax import lax
from jax.experimental import pallas as pl
from jax.experimental.pallas import tpu as pltpu
from jax.sharding import PartitionSpec as P

def path_of(sign):
    chips = [(y, 0) for y in range(4)] + [(y, 1) for y in (3, 2, 1, 0)]
    return [sign * y % 4 * 4 + xh * 2 + core for y, xh in chips for core in (0, 1)]


PATHS = path_of(1), path_of(-1)
PAIRS = [(0, 6), (1, 7), (2, 4), (3, 5)]
DT = 0.15
F32 = jnp.float32


def vmem():
    return pl.BlockSpec(memory_space=pltpu.VMEM)


def place_of():
    gy, gz = lax.axis_index("gy"), lax.axis_index("gz")
    y = lax.shift_right_logical(gy, 2)
    y = jnp.where(gz == 0, y, -y) & 3
    xh, core = lax.shift_right_logical(gy, 1) & 1, gy & 1
    return 2 * jnp.where(xh == 0, y, 7 - y) + core, core, gz


def owners():
    gz = lax.axis_index("gz")
    return [jnp.where(gz == 0, a, b) for a, b in zip(PATHS[0], PATHS[1][::-1])]


def component_copies(density, momentum, held, sems, outward):
    copies = []
    for c in range(4):
        far, near = density if c == 0 else momentum.at[c - 1], held.at[c]
        source, target = (near, far) if outward else (far, near)
        copies.append(pltpu.make_async_copy(source, target, sems.at[c]))
    return copies


def pack_kernel(density, momentum, send, held, packed, sems, send_sems):
    copies = component_copies(density, momentum, held, sems, False)
    for copy in copies:
        copy.start()
    to = owners()
    leaving = []
    for c in range(4):
        copies[c].wait()
        for q, (a, b) in enumerate(PAIRS):
            turned = jnp.concatenate([held[c, a], held[c, b]], axis=0).T
            for k, device in enumerate(to):
                packed[c, device, q] = turned[8 * k : 8 * k + 8]
        leaving.append(pltpu.make_async_copy(packed.at[c], send.at[:, c], send_sems.at[c]))
        leaving[c].start()
    for copy in leaving:
        copy.wait()


def unpack_kernel(recv, density, momentum, held, sems):
    copies = component_copies(density, momentum, held, sems, True)
    given = owners()
    for c in range(4):
        for q, (a, b) in enumerate(PAIRS):
            turned = jnp.concatenate([recv[device, c, q] for device in given], axis=0).T
            held[c, a] = turned[:64]
            held[c, b] = turned[64:]
        copies[c].start()
    for copy in copies:
        copy.wait()


def lanes():
    return lax.broadcasted_iota(jnp.int32, (8, 128), 1)


def ring_roll(tile, shift, lane):
    far, near = shift // 128, shift % 128
    turned = pltpu.roll(tile, near, 1)
    return jnp.where(lane < near, pltpu.roll(turned, far + 1, 0), pltpu.roll(turned, far, 0))


def ring_next(tile, lane):
    turned = pltpu.roll(tile, 127, 1)
    return jnp.where(lane == 127, pltpu.roll(turned, 7, 0), turned)


def ring_prev(tile, lane):
    turned = pltpu.roll(tile, 1, 1)
    return jnp.where(lane == 0, pltpu.roll(turned, 1, 0), turned)


def remap_kernel(table, weights, recv, rem, x_first, x_second, z_inner, z_outer, mixed, shifts, sem):
    fetch = pltpu.make_async_copy(table, shifts, sem)
    fetch.start()
    lane = lanes()
    _, core, gz = place_of()
    odd = (lax.axis_index("gx") & 1) == 1
    inner_is_high = (core ^ gz) == 0

    def mix(c, _):
        for q, columns in enumerate(PAIRS):
            weight = [weights[x] for x in columns]
            for z in range(8):
                base = (c * 4 + q) * 8 + z
                even = recv[pl.ds(base, 8, stride=256), :]
                odd = recv[pl.ds(base + 128, 8, stride=256), :]
                tiles = (
                    jnp.where(lane < 64, even, pltpu.roll(odd, 64, 1)),
                    jnp.where(lane < 64, pltpu.roll(even, 64, 1), odd),
                )
                for tile, w, x in zip(tiles, weight, columns):
                    mixed[c, x, z] = (1.0 - w) * tile + w * ring_prev(tile, lane)
        return 0

    lax.fori_loop(0, 4, mix, 0)
    fetch.wait()

    def move(c, _):
        leaving = {}
        for x in range(8):
            ends = []
            for z in range(8):
                value = ring_roll(mixed[c, x, z], shifts[x], lane)
                rem[c, x, z] = value
                if z < 2 or z >= 6:
                    ends.append(value)
                if x < 2:
                    leaving[x, z] = ring_roll(mixed[c, x, z], shifts[8 + x], lane)
                if x >= 6:
                    leaving[x, z] = ring_roll(mixed[c, x, z], shifts[4 + x], lane)
            for g in range(2):
                z_inner[c, x, g] = jnp.where(inner_is_high, ends[2 + g], ends[g])
                z_outer[c, x, g] = jnp.where(inner_is_high, ends[g], ends[2 + g])
        for x in range(2):
            for z in range(8):
                x_first[c, x, z] = jnp.where(odd, leaving[6 + x, z], leaving[x, z])
                x_second[c, x, z] = jnp.where(odd, leaving[x, z], leaving[6 + x, z])
        return 0

    lax.fori_loop(0, 4, move, 0)


def minmod(a, b):
    return jnp.maximum(jnp.minimum(a, b), 0.0) + jnp.minimum(jnp.maximum(a, b), 0.0)


def inverse(a):
    first = pl.reciprocal(a, approx=True)
    return first * (2.0 - a * first)


def predict(cell, below, above, k):
    slope = [minmod(below[c], above[c]) for c in range(4)]
    half = [0.5 * s for s in slope]
    minus = [cell[c] - half[c] for c in range(4)]
    plus = [cell[c] + half[c] for c in range(4)]
    v_minus = minus[k] * inverse(minus[0])
    v_plus = plus[k] * inverse(plus[0])
    change = [0.075 * slope[k]]
    for c in range(1, 4):
        term = plus[c] * v_plus - minus[c] * v_minus
        if c == k:
            term = term + slope[0]
        change.append(0.075 * term)
    return [minus[c] - change[c] for c in range(4)], [plus[c] - change[c] for c in range(4)]


def face_flux(left, right, k, v_left, v_right):
    slowest = jnp.minimum(jnp.minimum(v_left, v_right) - 1.0, 0.0)
    fastest = jnp.maximum(jnp.maximum(v_left, v_right) + 1.0, 0.0)
    scale = inverse(fastest - slowest)
    up = fastest * scale
    down = -slowest * scale
    mix = fastest * slowest * scale
    from_left = up * v_left - mix
    from_right = down * v_right + mix
    flux = [left[c] * from_left + right[c] * from_right for c in range(4)]
    flux[k] = flux[k] + (up * left[0] + down * right[0])
    return flux


def along(rem, acc):
    lane = lanes()
    place, _, gz = place_of()
    base = 128 * gz + 8 * jnp.where(gz == 0, place, 15 - place)
    level = base + lax.broadcasted_iota(jnp.int32, (8, 128), 0)
    height = (level.astype(F32) + (0.5 - 128.0)) * (1.0 / 128.0)

    def one(x, _):
        def rows(c, p):
            return pl.ds((c * 8 + x) * 64 + p, 8, stride=8)

        def upward(tiles):
            return [pltpu.roll(t, 1, 1) for t in tiles]

        def downward(tiles):
            return [pltpu.roll(t, 127, 1) for t in tiles]

        def first_from(here, before):
            return [jnp.where(lane == 0, b, h) for h, b in zip(here, before)]

        def last_from(here, after):
            return [jnp.where(lane == 127, b, h) for h, b in zip(here, after)]

        def load(p):
            return [rem[rows(c, p), :] for c in range(4)]

        def differ(p, before):
            cell = load(p)
            turned = upward(cell)
            below = [u - w for u, w in zip(cell, first_from(turned, before))]
            return cell, below, downward(below), turned

        def store(p, flux, before):
            cell = load(p)
            div = [f - w for f, w in zip(flux, before)]
            acc[rows(0, p), :] = cell[0] - DT * div[0]
            acc[rows(1, p), :] = cell[1] - DT * (div[1] - 2.0 * cell[2])
            acc[rows(2, p), :] = cell[2] - DT * (div[2] + 0.5 * cell[1])
            acc[rows(3, p), :] = cell[3] - DT * (div[3] + height * cell[0])

        state = differ(0, upward(load(7)))
        first_down = state[2]
        first_minus = first_flux = minus_before = plus_before = flux_turned = None
        for p in range(9):
            if p < 8:
                cell, below, down, turned = state
                if p < 7:
                    state = differ(p + 1, turned)
                above = last_from(down, state[2] if p < 7 else first_down)
                minus, plus = predict(cell, below, above, 2)
                minus_down = downward(minus)
                if p == 0:
                    first_minus = minus_down
            else:
                minus_down, plus = first_minus, None
            if p > 0:
                right = last_from(minus_before, minus_down)
                flux = face_flux(
                    plus_before,
                    right,
                    2,
                    plus_before[2] * inverse(plus_before[0]),
                    right[2] * inverse(right[0]),
                )
                up = upward(flux)
                if p == 1:
                    first_flux = flux, up
                else:
                    store(p - 1, flux, first_from(up, flux_turned))
                flux_turned = up
            minus_before, plus_before = minus_down, plus
        store(0, first_flux[0], first_from(first_flux[1], flux_turned))
        return 0

    lax.fori_loop(0, 8, one, 0, unroll=2)


def face(left, right, k):
    return face_flux(left, right, k, left[k] * inverse(left[0]), right[k] * inverse(right[0]))


def less(cell, flux):
    return [u - DT * f for u, f in zip(cell, flux)]


def more(cell, flux):
    return [u + DT * f for u, f in zip(cell, flux)]


def difference(upper, lower):
    return [a - b for a, b in zip(upper, lower)]


def march(cells, k):
    fluxes = []
    first_minus = plus_before = None
    below = difference(cells[1], cells[0])
    for i in range(1, 7):
        above = difference(cells[i + 1], cells[i])
        minus, plus = predict(cells[i], below, above, k)
        below = above
        if i == 1:
            first_minus = minus
        else:
            fluxes.append(face(plus_before, minus, k))
        plus_before = plus
    return fluxes, first_minus, plus_before


def low_end(ghosts, cells, minus, k):
    outside, inside = difference(ghosts[1], ghosts[0]), difference(cells[1], cells[0])
    between = difference(cells[0], ghosts[1])
    _, plus_ghost = predict(ghosts[1], outside, between, k)
    minus_cell, plus_cell = predict(cells[0], between, inside, k)
    return face(plus_ghost, minus_cell, k), face(plus_cell, minus, k)


def high_end(ghosts, cells, plus, k):
    outside, inside = difference(ghosts[1], ghosts[0]), difference(cells[1], cells[0])
    between = difference(ghosts[0], cells[1])
    minus_cell, plus_cell = predict(cells[1], inside, between, k)
    minus_ghost, _ = predict(ghosts[0], between, outside, k)
    return face(plus, minus_cell, k), face(plus_cell, minus_ghost, k)


def inside(acc, rem, part, x_minus, x_plus, z_minus, z_plus):
    def line(cells, values, k):
        fluxes, minus, plus = march(cells, k)
        values[1] = less(values[1], fluxes[0])
        for i in range(2, 6):
            values[i] = less(values[i], difference(fluxes[i - 1], fluxes[i - 2]))
        values[6] = more(values[6], fluxes[4])
        return values, minus, plus

    def radial(z, _):
        cells = [[rem[c, x, z] for c in range(4)] for x in range(8)]
        values = [
            [acc[pl.ds(pl.multiple_of(((c * 8 + x) * 8 + z) * 8, 8), 8), :] for c in range(4)]
            for x in range(8)
        ]
        values, minus, plus = line(cells, values, 1)
        for c in range(4):
            for x in range(8):
                part[c, x, z] = values[x][c]
            x_minus[c, z] = minus[c]
            x_plus[c, z] = plus[c]
        return 0

    def vertical(x, _):
        cells = [[rem[c, x, z] for c in range(4)] for z in range(8)]
        values = [[part[c, x, z] for c in range(4)] for z in range(8)]
        values, minus, plus = line(cells, values, 3)
        for c in range(4):
            for z in range(1, 7):
                part[c, x, z] = values[z][c]
            z_minus[c, x] = minus[c]
            z_plus[c, x] = plus[c]
        return 0

    lax.fori_loop(0, 8, radial, 0)
    lax.fori_loop(0, 8, vertical, 0)


def waits_long():
    return lax.axis_index("gx") == 0


def early_kernel(rem, rem_rows, x_first, x_second, z_inner, z_outer, *refs):
    part, x_minus, x_plus, z_minus, z_plus, first_out, second_out, inner_out, outer_out, acc = refs

    @pl.when(waits_long())
    def _():
        along(rem_rows, acc)
        inside(acc, rem, part, x_minus, x_plus, z_minus, z_plus)

    def pass_on(c, _):
        first_out[c] = x_first[c]
        second_out[c] = x_second[c]
        inner_out[c] = z_inner[c]
        outer_out[c] = z_outer[c]
        return 0

    lax.fori_loop(0, 4, pass_on, 0)


def late_kernel(rem, rem_rows, *refs):
    done, (*results, acc) = refs[:5], refs[5:]
    early = waits_long()

    @pl.when(early)
    def _():
        def pass_on(c, _):
            for given, result in zip(done, results):
                result[c] = given[c]
            return 0

        lax.fori_loop(0, 4, pass_on, 0)

    @pl.when(jnp.logical_not(early))
    def _():
        along(rem_rows, acc)
        inside(acc, rem, *results)


def radial_kernel(part, rem, x_minus, x_plus, from_first, from_second, ends):
    odd = (lax.axis_index("gx") & 1) == 1

    def one(z, _):
        def at(ref, x):
            return [ref[c, x, z] for c in range(4)]

        def ghosts(low):
            pairs = [zip(at(from_first, x), at(from_second, x)) for x in range(2)]
            return [[jnp.where(odd == low, b, a) for a, b in pair] for pair in pairs]

        below, above = low_end(
            ghosts(True),
            [at(rem, 0), at(rem, 1)],
            [x_minus[c, z] for c in range(4)],
            1,
        )
        values = [less(at(part, 0), difference(above, below)), more(at(part, 1), above)]
        below, above = high_end(
            ghosts(False),
            [at(rem, 6), at(rem, 7)],
            [x_plus[c, z] for c in range(4)],
            1,
        )
        values += [less(at(part, 6), below), less(at(part, 7), difference(above, below))]
        for i, value in enumerate(values):
            for c in range(4):
                ends[c, i, z] = value[c]
        return 0

    lax.fori_loop(0, 8, one, 0)


def vertical_kernel(part, ends, rem, z_minus, z_plus, from_outer, from_inner, send):
    lane = lanes()
    place, core, gz = place_of()
    inner_is_high = (core ^ gz) == 0
    at_end = place == 0

    def column(x, values):
        def at(z):
            return [rem[c, x, z] for c in range(4)]

        cells = {z: at(z) for z in (0, 1, 6, 7)}
        low, high = [], []
        for g in range(2):
            near = [from_inner[c, x, g] for c in range(4)]
            far = [from_outer[c, x, g] for c in range(4)]
            end = [jnp.where(inner_is_high, a, b) for a, b in zip(cells[0], cells[7])]
            far = [jnp.where(at_end, a, b) for a, b in zip(end, far)]
            low.append([jnp.where(inner_is_high, a, b) for a, b in zip(far, near)])
            high.append([jnp.where(inner_is_high, a, b) for a, b in zip(near, far)])
        below, above = low_end(low, [cells[0], cells[1]], [z_minus[c, x] for c in range(4)], 3)
        values[0], values[1] = less(values[0], difference(above, below)), more(values[1], above)
        below, above = high_end(high, [cells[6], cells[7]], [z_plus[c, x] for c in range(4)], 3)
        values[6], values[7] = less(values[6], below), less(values[7], difference(above, below))
        return values

    def pack(q, first, second):
        for z in range(8):
            for c in range(4):
                base = (c * 4 + q) * 8 + z
                a, b = first[z][c], second[z][c]
                send[pl.ds(base, 8, stride=256), :] = jnp.where(lane < 64, a, pltpu.roll(b, 64, 1))
                send[pl.ds(base + 128, 8, stride=256), :] = jnp.where(lane < 64, pltpu.roll(a, 64, 1), b)

    def outer_pair(q, _):
        pair = [
            column(x, [[ends[c, i, z] for c in range(4)] for z in range(8)])
            for x, i in ((q, q), (q + 6, q + 2))
        ]
        pack(q, *pair)
        return 0

    def inner_pair(q, _):
        pair = [column(x, [[part[c, x, z] for c in range(4)] for z in range(8)]) for x in (q, q + 2)]
        pack(q, *pair)
        return 0

    lax.fori_loop(0, 2, outer_pair, 0)
    lax.fori_loop(2, 4, inner_pair, 0)


def kernel_call(kernel, name, given, results, scratch=(), spaces=None, out_spaces=None, limit=48):
    return pl.pallas_call(
        kernel,
        out_shape=results,
        in_specs=spaces or [vmem()] * len(given),
        out_specs=out_spaces or (vmem(),) * len(results),
        scratch_shapes=list(scratch),
        compiler_params=pltpu.CompilerParams(vmem_limit_bytes=limit << 20),
        cost_estimate=pl.CostEstimate(flops=1000, bytes_accessed=1000, transcendentals=0),
        name=name,
    )(*given)


def on_device(density, momentum, column_shift, column_fraction, shear_offset):
    tile = lambda *lead: jax.ShapeDtypeStruct(lead + (8, 128), F32)
    far = pl.BlockSpec(memory_space=pl.ANY)
    moving = [pltpu.VMEM((4, 8, 64, 128), F32), pltpu.SemaphoreType.DMA((4,))]
    (send,) = kernel_call(
        pack_kernel,
        "pack",
        (density, momentum),
        (tile(16, 4, 4),),
        [
            moving[0],
            pltpu.VMEM((4, 16, 4, 8, 128), F32),
            moving[1],
            pltpu.SemaphoreType.DMA((4,)),
        ],
        spaces=[far, far],
        out_spaces=(far,),
        limit=60,
    )
    recv = lax.all_to_all(send, "gy", 0, 0)
    gx, offset = lax.axis_index("gx"), shear_offset[0]
    shifts = lax.dynamic_slice(column_shift, (8 * gx,), (8,))
    leaving = jnp.concatenate(
        [shifts[:2] - jnp.where(gx == 0, offset, 0), shifts[6:] + jnp.where(gx == 7, offset, 0)]
    )
    table = jnp.concatenate([shifts, leaving & 1023, jnp.zeros((116,), jnp.int32)])
    weights = lax.dynamic_slice(column_fraction, (8 * gx,), (8,))
    weights = jnp.broadcast_to(weights[:, None, None], (8, 8, 128))
    rem, x_first, x_second, z_inner, z_outer = kernel_call(
        remap_kernel,
        "remap",
        (table, weights, recv.reshape(2048, 128)),
        (tile(4, 8, 8), tile(4, 2, 8), tile(4, 2, 8), tile(4, 8, 2), tile(4, 8, 2)),
        [
            pltpu.VMEM((4, 8, 8, 8, 128), F32),
            pltpu.SMEM((128,), jnp.int32),
            pltpu.SemaphoreType.DMA,
        ],
        spaces=[far, vmem(), vmem()],
    )
    results = (tile(4, 8, 8),) + (tile(4, 8),) * 4
    rows = rem.reshape(2048, 128)
    *early, x_first, x_second, z_inner, z_outer = kernel_call(
        early_kernel,
        "early",
        (rem, rows, x_first, x_second, z_inner, z_outer),
        results + (tile(4, 2, 8), tile(4, 2, 8), tile(4, 8, 2), tile(4, 8, 2)),
        [pltpu.VMEM((2048, 128), F32)],
    )
    from_first = lax.ppermute(x_first, "gx", [(i, ((i - 1) ^ 1) + 1 & 7) for i in range(8)])
    from_second = lax.ppermute(x_second, "gx", [(i, i ^ 1) for i in range(8)])
    from_inner = lax.ppermute(z_inner, "gy", [(i, i ^ 1) for i in range(16)])
    outer = [(2 * a + g, 2 * b + g) for g in (0, 1) for a, b in zip(PATHS[g][1:-1:2], PATHS[g][2:-1:2])]
    outer.append((2 * PATHS[0][-1], 2 * PATHS[1][-1] + 1))
    from_outer = lax.ppermute(z_outer, ("gy", "gz"), outer + [(b, a) for a, b in outer])

    part, x_minus, x_plus, z_minus, z_plus = kernel_call(
        late_kernel, "late", (rem, rows, *early), results, [pltpu.VMEM((2048, 128), F32)]
    )
    (ends,) = kernel_call(
        radial_kernel, "radial", (part, rem, x_minus, x_plus, from_first, from_second), (tile(4, 4, 8),)
    )
    (send,) = kernel_call(
        vertical_kernel,
        "vertical",
        (part, ends, rem, z_minus, z_plus, from_outer, from_inner),
        (jax.ShapeDtypeStruct((2048, 128), F32),),
    )
    recv = lax.all_to_all(send.reshape(16, 4, 4, 8, 128), "gy", 0, 0)
    return kernel_call(
        unpack_kernel,
        "unpack",
        (recv,),
        (jax.ShapeDtypeStruct(density.shape, F32), jax.ShapeDtypeStruct(momentum.shape, F32)),
        moving,
        out_spaces=(far, far),
    )


def solution(mesh):
    in_specs = (P("gx", "gy", "gz"), P(None, "gx", "gy", "gz"), P(), P(), P())
    out_specs = (P("gx", "gy", "gz"), P(None, "gx", "gy", "gz"))
    return jax.shard_map(
        on_device, mesh=mesh, in_specs=in_specs, out_specs=out_specs, check_vma=False
    )
```

profile of v0, /device:TPU:1, one launch (start us, length us, event | category | flops | bytes accessed | tf_op | source)
XLA Modules:
  0.0 68.2 jit_solution(10867834822708738627)
XLA Ops:
  0.6 2.3 %pack.1 = f32[16,4,4,8,128]{4,3,2,1,0:T(8,128)} custom-call(f32[8,64,128]{2,1,0:T(8,128)} %density.1, f32[3,8,64,128]{3,2,1,0:T(8,128)} %momentum.1), custom_call_target="tpu_custom_call" | custom-call | flops 1000 | bytes 1000 | tf_op jit(solution)/shard_map/pack/pallas_call | solution.py:474
  2.9 8.5 %all-to-all-start = ((f32[16,4,4,8,128]{4,3,2,1,0:T(8,128)}), f32[16,4,4,8,128]{4,3,2,1,0:T(8,128)S(1)}, u32[]{:S(2)}, u32[]{:S(2)}) async-start(f32[16,4,4,8,128]{4,3,2,1,0:T(8,128)} %pack.1), calls=%async_computation | async-start | bytes 2097152 | tf_op jit(solution)/shard_map/all_to_all | solution.py:505
  12.0 0.0 copy-start
  12.0 0.6 copy-done
  12.7 0.0 copy-start.1
  12.7 0.1 dynamic_slice.6
  12.8 0.6 copy-done.1
  13.3 0.1 dynamic_slice.7
  13.4 0.1 slice_subtract_fusion
  13.5 0.1 add_and_fusion
  13.6 0.1 pad_add_fusion.table
  13.6 14.9 %all-to-all-done = f32[16,4,4,8,128]{4,3,2,1,0:T(8,128)S(1)} async-done(((f32[16,4,4,8,128]{4,3,2,1,0:T(8,128)}), f32[16,4,4,8,128]{4,3,2,1,0:T(8,128)S(1)}, u32[]{:S(2)}, u32[]{:S(2)}) %all-to-all-start) | async-done | bytes 1048608 | tf_op jit(solution)/shard_map/all_to_all | solution.py:505
  28.6 0.1 broadcast_in_dim.10.weights
  28.7 1.9 %remap.1 = (f32[4,8,8,8,128]{4,3,2,1,0:T(8,128)S(1)}, f32[4,2,8,8,128]{4,3,2,1,0:T(8,128)S(1)}, f32[4,2,8,8,128]{4,3,2,1,0:T(8,128)S(1)}, f32[4,8,2,8,128]{4,3,2,1,0:T(8,128)S(1)}, f32[4,8,2,8,128]{4,3,2,1,0:T(8,128)S(1)}) custom-call(s32[128]{0:T(128)S(1)} %pad_add_fusion.table, f32[8,8,128]{2,1,0:T(8,128)S(1)} %broadcast_in_dim.10.weights, ...), custom_call_target="tpu_custom_call" | custom-call | flops 1000 | bytes 1000 | tf_op jit(solution)/shard_map/remap/pallas_call | solution.py:474
  30.6 4.2 %early.1 = (f32[4,8,8,8,128]{4,3,2,1,0:T(8,128)S(1)}, f32[4,8,8,128]{3,2,1,0:T(8,128)S(1)}, f32[4,8,8,128]{3,2,1,0:T(8,128)S(1)}, f32[4,8,8,128]{3,2,1,0:T(8,128...) custom-call(f32[4,8,8,8,128]{4,3,2,1,0:T(8,128)S(1)} %get-tuple-elem, ...), custom_call_target="tpu_custom_call" | custom-call | flops 1000 | bytes 1000 | tf_op jit(solution)/shard_map/early/pallas_call | solution.py:474
  34.7 1.6 %collective-permute-start = (f32[4,2,8,8,128]{4,3,2,1,0:T(8,128)S(1)}, f32[4,2,8,8,128]{4,3,2,1,0:T(8,128)S(1)}, u32[]{:S(2)}, u32[]{:S(2)}) collective-permute-start(f32[4,2,8,8,128]{4,3,2,1,0:T(8,128)S(1)} %get-tuple-element.34), channel_id=1, source_target_pairs={{0,224},{32,64},{64,32},{96,128},{128,96},{160,192},{192,160},{224... | collective-permute-start | bytes 786440 | tf_op jit(solution)/shard_map/ppermute | solution.py:535
  36.3 0.0 collective-permute-start.1
  36.3 2.0 %collective-permute-start.2 = (f32[4,8,2,8,128]{4,3,2,1,0:T(8,128)S(1)}, f32[4,8,2,8,128]{4,3,2,1,0:T(8,128)S(1)}, u32[]{:S(2)}, u32[]{:S(2)}) collective-permute-start(f32[4,8,2,8,128]{4,3,2,1,0:T(8,128)S(1)} %get-tuple-element.38), channel_id=1, source_target_pairs={{2,8},{10,16},{18,24},{26,28},{30,20},{22,12},{14,4},{3,25},{27,17... | collective-permute-start | bytes 786440 | tf_op jit(solution)/shard_map/ppermute | solution.py:540
  38.4 0.1 collective-permute-start.3
  38.5 0.1 late.1
  38.6 4.4 %collective-permute-done.from_first = f32[4,2,8,8,128]{4,3,2,1,0:T(8,128)S(1)} collective-permute-done((f32[4,2,8,8,128]{4,3,2,1,0:T(8,128)S(1)}, f32[4,2,8,8,128]{4,3,2,1,0:T(8,128)S(1)}, u32[]{:S(2)}, u32[]{:S(2)}) %collective-permute-start) | collective-permute-done | bytes 262176 | tf_op jit(solution)/shard_map/ppermute | solution.py:535
  42.9 0.0 collective-permute-done.1.from_second
  42.9 0.7 %radial.1.ends = f32[4,4,8,8,128]{4,3,2,1,0:T(8,128)S(1)} custom-call(f32[4,8,8,8,128]{4,3,2,1,0:T(8,128)S(1)} %get-tuple-element.31.part, f32[4,8,8,8,128]{4,3,2,1,0:T(8,128)S(1)} %get-tuple-element.21.rem, f32[4,8,8,128]{3,2,1,0:T(8,128)S(1)} %get-tuple-element.32.x_minus, f32[4,8,8,128]{3,2,1,0:T(8,128)S(1)} %get-tuple-element.33.x_plus, ...), custom_call_target="tpu_custom_call" | custom-call | flops 1000 | bytes 1000 | tf_op jit(solution)/shard_map/radial/pallas_call | solution.py:474
  43.7 0.7 collective-permute-done.2.from_outer
  44.3 0.0 collective-permute-done.3.from_inner
  44.3 1.6 %vertical.1 = f32[2048,128]{1,0:T(8,128)S(1)} custom-call(f32[4,8,8,8,128]{4,3,2,1,0:T(8,128)S(1)} %get-tuple-element.31.part, f32[4,4,8,8,128]{4,3,2,1,0:T(8,128)S(1)} %radial.1.ends, f32[4,8,8,8,128]{4,3,2,1,0:T(8,128)S(1)} %get-tuple-element.21.rem, f32[4,8,8,128]{3,2,1,0:T(8,128)S(1)} %get-tuple-element.36.z_minus, ...), custom_call_target="tpu_custom_call" | custom-call | flops 1000 | bytes 1000 | tf_op jit(solution)/shard_map/vertical/pallas_call | solution.py:474
  45.9 21.2 %all_to_all.10.recv = f32[16,4,4,8,128]{4,3,2,1,0:T(8,128)S(1)} all-to-all(f32[16,4,4,8,128]{4,3,2,1,0:T(8,128)S(1)} %bitcast.8), channel_id=1, replica_groups=mesh['gx'=8,'gy'=16,'gz'=2] {'gy'}, dimensions={0} | all-to-all | bytes 2097152 | tf_op jit(solution)/shard_map/all_to_all | solution.py:554
  67.1 1.1 %unpack.1 = (f32[8,64,128]{2,1,0:T(8,128)}, f32[3,8,64,128]{3,2,1,0:T(8,128)}) custom-call(f32[16,4,4,8,128]{4,3,2,1,0:T(8,128)S(1)} %all_to_all.10.recv), custom_call_target="tpu_custom_call" | custom-call | flops 1000 | bytes 1000 | tf_op jit(solution)/shard_map/unpack/pallas_call | solution.py:474
  (1 shorter events, 0.0 us)
Async XLA Ops:
  2.9 25.7 %all-to-all-start = ((f32[16,4,4,8,128]{4,3,2,1,0:T(8,128)}), f32[16,4,4,8,128]{4,3,2,1,0:T(8,128)S(1)}, u32[]{:S(2)}, u32[]{:S(2)}) async-start(f32[16,4,4,8,128]{4,3,2,1,0:T(8,128)} %pack.1), calls=%async_computation | async-start | bytes 2097152 | tf_op jit(solution)/shard_map/all_to_all | solution.py:505
  12.0 0.7 copy-start
  12.7 0.7 copy-start.1
  34.7 8.2 %collective-permute-start = (f32[4,2,8,8,128]{4,3,2,1,0:T(8,128)S(1)}, f32[4,2,8,8,128]{4,3,2,1,0:T(8,128)S(1)}, u32[]{:S(2)}, u32[]{:S(2)}) collective-permute-start(f32[4,2,8,8,128]{4,3,2,1,0:T(8,128)S(1)} %get-tuple-element.34), channel_id=1, source_target_pairs={{0,224},{32,64},{64,32},{96,128},{128,96},{160,192},{192,160},{224... | collective-permute-start | bytes 786440 | tf_op jit(solution)/shard_map/ppermute | solution.py:535
  36.3 6.6 %collective-permute-start.1 = (f32[4,2,8,8,128]{4,3,2,1,0:T(8,128)S(1)}, f32[4,2,8,8,128]{4,3,2,1,0:T(8,128)S(1)}, u32[]{:S(2)}, u32[]{:S(2)}) collective-permute-start(f32[4,2,8,8,128]{4,3,2,1,0:T(8,128)S(1)} %get-tuple-element.35), channel_id=1, source_target_pairs={{0,32},{32,0},{64,96},{96,64},{128,160},{160,128},{192,224},{224,1... | collective-permute-start | bytes 786440 | tf_op jit(solution)/shard_map/ppermute | solution.py:536
  36.3 8.0 %collective-permute-start.2 = (f32[4,8,2,8,128]{4,3,2,1,0:T(8,128)S(1)}, f32[4,8,2,8,128]{4,3,2,1,0:T(8,128)S(1)}, u32[]{:S(2)}, u32[]{:S(2)}) collective-permute-start(f32[4,8,2,8,128]{4,3,2,1,0:T(8,128)S(1)} %get-tuple-element.38), channel_id=1, source_target_pairs={{2,8},{10,16},{18,24},{26,28},{30,20},{22,12},{14,4},{3,25},{27,17... | collective-permute-start | bytes 786440 | tf_op jit(solution)/shard_map/ppermute | solution.py:540
  38.4 6.0 %collective-permute-start.3 = (f32[4,8,2,8,128]{4,3,2,1,0:T(8,128)S(1)}, f32[4,8,2,8,128]{4,3,2,1,0:T(8,128)S(1)}, u32[]{:S(2)}, u32[]{:S(2)}) collective-permute-start(f32[4,8,2,8,128]{4,3,2,1,0:T(8,128)S(1)} %get-tuple-element.39), channel_id=1, source_target_pairs={{0,2},{2,0},{4,6},{6,4},{8,10},{10,8},{12,14},{14,12},{16,18},{18,... | collective-permute-start | bytes 786440 | tf_op jit(solution)/shard_map/ppermute | solution.py:537
where the time goes:
time: 68.5 us; the launch traced here: 68.2 us
  blocking collectives  21.2 us (31%)
  waiting for transfers between devices  20 us (29%)
  starting transfers between devices  12.1 us (18%)
  Pallas kernels  11.9 us (17%)
  local copies, waits for them, and re-layouts  1.45 us (2%)
  between operations  1.36 us (2%)
    all_to_all x1, blocking collectives, on_device(): recv = lax.all_to_all(send.reshape(16, 4, 4, 8, 128), 'gy', 0, 0)  21.2 us
    all_to_all x1, waiting for transfers between devices, on_device(): recv = lax.all_to_all(send, 'gy', 0, 0)  14.9 us
    pallas_call x7, Pallas kernels, kernel_call(): pl.pallas_call(kernel, out_shape=results, in_specs=spaces or [vmem()] * l...  11.9 us
    all_to_all x1, starting transfers between devices, on_device(): recv = lax.all_to_all(send, 'gy', 0, 0)  8.46 us
    ppermute x1, waiting for transfers between devices, on_device(): lax.ppermute(x_first, 'gx', [(i, (i - 1 ^ 1) + 1 & 7) for i in range(8)])  4.35 us
    ppermute x1, starting transfers between devices, on_device(): lax.ppermute(z_outer, ('gy', 'gz'), outer + [(b, a) for a, b in outer])  2 us
    ppermute x1, starting transfers between devices, on_device(): lax.ppermute(x_first, 'gx', [(i, (i - 1 ^ 1) + 1 & 7) for i in range(8)])  1.59 us
  transfers between devices with their start and end apart: 5, of which 3 were waited for; matrix products, arithmetic and copies ran while one was open for 1% of the time, Pallas kernels for 1%

commit v1 on v0

--- a/solution.py
+++ b/solution.py
@@ -342,8 +342,8 @@
             z_plus[c, x] = plus[c]
         return 0
 
-    lax.fori_loop(0, 8, radial, 0)
-    lax.fori_loop(0, 8, vertical, 0)
+    lax.fori_loop(0, 8, radial, 0, unroll=2)
+    lax.fori_loop(0, 8, vertical, 0, unroll=2)
 
 
 def waits_long():
@@ -417,7 +417,7 @@
                 ends[c, i, z] = value[c]
         return 0
 
-    lax.fori_loop(0, 8, one, 0)
+    lax.fori_loop(0, 8, one, 0, unroll=2)
 
 
 def vertical_kernel(part, ends, rem, z_minus, z_plus, from_outer, from_inner, send):

time: 68.5 us -> 68.4 us (level)
  transfers between devices with their start and end apart: 5 -> 5, of which waited for: 3 -> 4; matrix products, arithmetic and copies ran while one was open for 1% -> 1% of each run, Pallas kernels for 1% -> 1%
where the time goes in v1:
time: 68.4 us; the launch traced here: 68.2 us
  blocking collectives  21.1 us (31%)
  waiting for transfers between devices  20 us (29%)
  starting transfers between devices  12.2 us (18%)
  Pallas kernels  11.8 us (17%)
  local copies, waits for them, and re-layouts  1.45 us (2%)
  between operations  1.36 us (2%)
    all_to_all x1, blocking collectives, on_device(): recv = lax.all_to_all(send.reshape(16, 4, 4, 8, 128), 'gy', 0, 0)  21.1 us
    all_to_all x1, waiting for transfers between devices, on_device(): recv = lax.all_to_all(send, 'gy', 0, 0)  14.9 us
    pallas_call x7, Pallas kernels, kernel_call(): pl.pallas_call(kernel, out_shape=results, in_specs=spaces or [vmem()] * l...  11.8 us
    all_to_all x1, starting transfers between devices, on_device(): recv = lax.all_to_all(send, 'gy', 0, 0)  8.46 us
    ppermute x1, waiting for transfers between devices, on_device(): lax.ppermute(x_first, 'gx', [(i, (i - 1 ^ 1) + 1 & 7) for i in range(8)])  4.27 us
    ppermute x1, starting transfers between devices, on_device(): lax.ppermute(z_outer, ('gy', 'gz'), outer + [(b, a) for a, b in outer])  2 us
    ppermute x1, starting transfers between devices, on_device(): lax.ppermute(x_first, 'gx', [(i, (i - 1 ^ 1) + 1 & 7) for i in range(8)])  1.68 us
  transfers between devices with their start and end apart: 5, of which 4 were waited for; matrix products, arithmetic and copies ran while one was open for 1% of the time, Pallas kernels for 1%

profile of v1, /device:TPU:1, one launch (start us, length us, event | category | flops | bytes accessed | tf_op | source)
XLA Modules:
  0.0 68.2 jit_solution(530662988001981210)
XLA Ops:
  0.6 2.3 %pack.1 = f32[16,4,4,8,128]{4,3,2,1,0:T(8,128)} custom-call(f32[8,64,128]{2,1,0:T(8,128)} %density.1, f32[3,8,64,128]{3,2,1,0:T(8,128)} %momentum.1), custom_call_target="tpu_custom_call" | custom-call | flops 1000 | bytes 1000 | tf_op jit(solution)/shard_map/pack/pallas_call | solution.py:474
  2.9 8.5 %all-to-all-start = ((f32[16,4,4,8,128]{4,3,2,1,0:T(8,128)}), f32[16,4,4,8,128]{4,3,2,1,0:T(8,128)S(1)}, u32[]{:S(2)}, u32[]{:S(2)}) async-start(f32[16,4,4,8,128]{4,3,2,1,0:T(8,128)} %pack.1), calls=%async_computation | async-start | bytes 2097152 | tf_op jit(solution)/shard_map/all_to_all | solution.py:505
  12.0 0.0 copy-start
  12.0 0.6 copy-done
  12.7 0.0 copy-start.1
  12.7 0.1 dynamic_slice.6
  12.8 0.6 copy-done.1
  13.3 0.1 dynamic_slice.7
  13.4 0.1 slice_subtract_fusion
  13.5 0.1 add_and_fusion
  13.6 0.1 pad_add_fusion.table
  13.6 14.9 %all-to-all-done = f32[16,4,4,8,128]{4,3,2,1,0:T(8,128)S(1)} async-done(((f32[16,4,4,8,128]{4,3,2,1,0:T(8,128)}), f32[16,4,4,8,128]{4,3,2,1,0:T(8,128)S(1)}, u32[]{:S(2)}, u32[]{:S(2)}) %all-to-all-start) | async-done | bytes 1048608 | tf_op jit(solution)/shard_map/all_to_all | solution.py:505
  28.6 0.1 broadcast_in_dim.10.weights
  28.7 1.9 %remap.1 = (f32[4,8,8,8,128]{4,3,2,1,0:T(8,128)S(1)}, f32[4,2,8,8,128]{4,3,2,1,0:T(8,128)S(1)}, f32[4,2,8,8,128]{4,3,2,1,0:T(8,128)S(1)}, f32[4,8,2,8,128]{4,3,2,1,0:T(8,128)S(1)}, f32[4,8,2,8,128]{4,3,2,1,0:T(8,128)S(1)}) custom-call(s32[128]{0:T(128)S(1)} %pad_add_fusion.table, f32[8,8,128]{2,1,0:T(8,128)S(1)} %broadcast_in_dim.10.weights, ...), custom_call_target="tpu_custom_call" | custom-call | flops 1000 | bytes 1000 | tf_op jit(solution)/shard_map/remap/pallas_call | solution.py:474
  30.6 4.1 %early.1 = (f32[4,8,8,8,128]{4,3,2,1,0:T(8,128)S(1)}, f32[4,8,8,128]{3,2,1,0:T(8,128)S(1)}, f32[4,8,8,128]{3,2,1,0:T(8,128)S(1)}, f32[4,8,8,128]{3,2,1,0:T(8,128...) custom-call(f32[4,8,8,8,128]{4,3,2,1,0:T(8,128)S(1)} %get-tuple-elem, ...), custom_call_target="tpu_custom_call" | custom-call | flops 1000 | bytes 1000 | tf_op jit(solution)/shard_map/early/pallas_call | solution.py:474
  34.7 1.7 %collective-permute-start = (f32[4,2,8,8,128]{4,3,2,1,0:T(8,128)S(1)}, f32[4,2,8,8,128]{4,3,2,1,0:T(8,128)S(1)}, u32[]{:S(2)}, u32[]{:S(2)}) collective-permute-start(f32[4,2,8,8,128]{4,3,2,1,0:T(8,128)S(1)} %get-tuple-element.34), channel_id=1, source_target_pairs={{0,224},{32,64},{64,32},{96,128},{128,96},{160,192},{192,160},{224... | collective-permute-start | bytes 786440 | tf_op jit(solution)/shard_map/ppermute | solution.py:535
  36.3 0.0 collective-permute-start.1
  36.3 2.0 %collective-permute-start.2 = (f32[4,8,2,8,128]{4,3,2,1,0:T(8,128)S(1)}, f32[4,8,2,8,128]{4,3,2,1,0:T(8,128)S(1)}, u32[]{:S(2)}, u32[]{:S(2)}) collective-permute-start(f32[4,8,2,8,128]{4,3,2,1,0:T(8,128)S(1)} %get-tuple-element.38), channel_id=1, source_target_pairs={{2,8},{10,16},{18,24},{26,28},{30,20},{22,12},{14,4},{3,25},{27,17... | collective-permute-start | bytes 786440 | tf_op jit(solution)/shard_map/ppermute | solution.py:540
  38.4 0.1 collective-permute-start.3
  38.5 0.1 late.1
  38.6 4.3 %collective-permute-done.from_first = f32[4,2,8,8,128]{4,3,2,1,0:T(8,128)S(1)} collective-permute-done((f32[4,2,8,8,128]{4,3,2,1,0:T(8,128)S(1)}, f32[4,2,8,8,128]{4,3,2,1,0:T(8,128)S(1)}, u32[]{:S(2)}, u32[]{:S(2)}) %collective-permute-start) | collective-permute-done | bytes 262176 | tf_op jit(solution)/shard_map/ppermute | solution.py:535
  42.9 0.1 collective-permute-done.1.from_second
  42.9 0.6 radial.1.ends
  43.6 0.7 %collective-permute-done.2.from_outer = f32[4,8,2,8,128]{4,3,2,1,0:T(8,128)S(1)} collective-permute-done((f32[4,8,2,8,128]{4,3,2,1,0:T(8,128)S(1)}, f32[4,8,2,8,128]{4,3,2,1,0:T(8,128)S(1)}, u32[]{:S(2)}, u32[]{:S(2)}) %collective-permute-start.2) | collective-permute-done | bytes 262176 | tf_op jit(solution)/shard_map/ppermute | solution.py:540
  44.3 0.0 collective-permute-done.3.from_inner
  44.3 1.6 %vertical.1 = f32[2048,128]{1,0:T(8,128)S(1)} custom-call(f32[4,8,8,8,128]{4,3,2,1,0:T(8,128)S(1)} %get-tuple-element.31.part, f32[4,4,8,8,128]{4,3,2,1,0:T(8,128)S(1)} %radial.1.ends, f32[4,8,8,8,128]{4,3,2,1,0:T(8,128)S(1)} %get-tuple-element.21.rem, f32[4,8,8,128]{3,2,1,0:T(8,128)S(1)} %get-tuple-element.36.z_minus, ...), custom_call_target="tpu_custom_call" | custom-call | flops 1000 | bytes 1000 | tf_op jit(solution)/shard_map/vertical/pallas_call | solution.py:474
  45.9 21.1 %all_to_all.10.recv = f32[16,4,4,8,128]{4,3,2,1,0:T(8,128)S(1)} all-to-all(f32[16,4,4,8,128]{4,3,2,1,0:T(8,128)S(1)} %bitcast.8), channel_id=1, replica_groups=mesh['gx'=8,'gy'=16,'gz'=2] {'gy'}, dimensions={0} | all-to-all | bytes 2097152 | tf_op jit(solution)/shard_map/all_to_all | solution.py:554
  67.0 1.1 %unpack.1 = (f32[8,64,128]{2,1,0:T(8,128)}, f32[3,8,64,128]{3,2,1,0:T(8,128)}) custom-call(f32[16,4,4,8,128]{4,3,2,1,0:T(8,128)S(1)} %all_to_all.10.recv), custom_call_target="tpu_custom_call" | custom-call | flops 1000 | bytes 1000 | tf_op jit(solution)/shard_map/unpack/pallas_call | solution.py:474
  (1 shorter events, 0.0 us)
Async XLA Ops:
  2.9 25.7 %all-to-all-start = ((f32[16,4,4,8,128]{4,3,2,1,0:T(8,128)}), f32[16,4,4,8,128]{4,3,2,1,0:T(8,128)S(1)}, u32[]{:S(2)}, u32[]{:S(2)}) async-start(f32[16,4,4,8,128]{4,3,2,1,0:T(8,128)} %pack.1), calls=%async_computation | async-start | bytes 2097152 | tf_op jit(solution)/shard_map/all_to_all | solution.py:505
  12.0 0.7 copy-start
  12.7 0.7 copy-start.1
  34.7 8.2 %collective-permute-start = (f32[4,2,8,8,128]{4,3,2,1,0:T(8,128)S(1)}, f32[4,2,8,8,128]{4,3,2,1,0:T(8,128)S(1)}, u32[]{:S(2)}, u32[]{:S(2)}) collective-permute-start(f32[4,2,8,8,128]{4,3,2,1,0:T(8,128)S(1)} %get-tuple-element.34), channel_id=1, source_target_pairs={{0,224},{32,64},{64,32},{96,128},{128,96},{160,192},{192,160},{224... | collective-permute-start | bytes 786440 | tf_op jit(solution)/shard_map/ppermute | solution.py:535
  36.3 6.6 %collective-permute-start.1 = (f32[4,2,8,8,128]{4,3,2,1,0:T(8,128)S(1)}, f32[4,2,8,8,128]{4,3,2,1,0:T(8,128)S(1)}, u32[]{:S(2)}, u32[]{:S(2)}) collective-permute-start(f32[4,2,8,8,128]{4,3,2,1,0:T(8,128)S(1)} %get-tuple-element.35), channel_id=1, source_target_pairs={{0,32},{32,0},{64,96},{96,64},{128,160},{160,128},{192,224},{224,1... | collective-permute-start | bytes 786440 | tf_op jit(solution)/shard_map/ppermute | solution.py:536
  36.3 8.0 %collective-permute-start.2 = (f32[4,8,2,8,128]{4,3,2,1,0:T(8,128)S(1)}, f32[4,8,2,8,128]{4,3,2,1,0:T(8,128)S(1)}, u32[]{:S(2)}, u32[]{:S(2)}) collective-permute-start(f32[4,8,2,8,128]{4,3,2,1,0:T(8,128)S(1)} %get-tuple-element.38), channel_id=1, source_target_pairs={{2,8},{10,16},{18,24},{26,28},{30,20},{22,12},{14,4},{3,25},{27,17... | collective-permute-start | bytes 786440 | tf_op jit(solution)/shard_map/ppermute | solution.py:540
  38.4 6.0 %collective-permute-start.3 = (f32[4,8,2,8,128]{4,3,2,1,0:T(8,128)S(1)}, f32[4,8,2,8,128]{4,3,2,1,0:T(8,128)S(1)}, u32[]{:S(2)}, u32[]{:S(2)}) collective-permute-start(f32[4,8,2,8,128]{4,3,2,1,0:T(8,128)S(1)} %get-tuple-element.39), channel_id=1, source_target_pairs={{0,2},{2,0},{4,6},{6,4},{8,10},{10,8},{12,14},{14,12},{16,18},{18,... | collective-permute-start | bytes 786440 | tf_op jit(solution)/shard_map/ppermute | solution.py:537
